TPU v7x, 32 devices: a whole 2x2x4 slice. The times are simulated.
32 devices in a mesh: grp: 4 (over z), dom: 8 (over y, x, core).
Axes of the slice: x: 2, y: 2, z: 4, core: 2. Of those that a mesh axis runs over, the one named last changes fastest.
Arguments:
- leaf_load: bfloat16 [8, 4, 1024, 128], P('dom', 'grp'), may hold values from -6 to 6
- leaf_map: bfloat16 [8, 4, 1024, 1024], P('dom', 'grp'), may hold values from -0.1875 to 0.1875
- group_map: bfloat16 [8, 4096, 4096], P('dom', 'grp'), may hold values from -0.09375 to 0.09375
- node_index: int32 [8, 4, 1024], P('dom', 'grp'), may hold values from 0 to 4095, as said below
- west_coupling: float32 [8, 256, 256], P('dom'), may hold values from -1.5 to 1.5
- east_coupling: float32 [8, 256, 256], P('dom'), may hold values from -1.5 to 1.5
Outputs:
- leaf_solution: bfloat16 [8, 4, 1024, 128], P('dom', 'grp')
Inputs may be any that keep to these rules, and one draw needn't show every extreme that they name: `node_index`: each leaf's list names 1024 different interface nodes of its group.
All inputs are finite; a program needn't handle non-finite values.
Results may differ from a plain program's by a relative error of at most 0.015.
Values may be sent and summed in bfloat16 or wider, within the bound.
A program may use at most 128 MiB of HBM per device.

v0:
```python
import jax
import jax.numpy as jnp
from jax import lax
from jax.sharding import PartitionSpec as P


def carried_in(part, axis, combine, identity, reverse):
    count = lax.axis_size(axis)
    place = lax.axis_index(axis)
    ahead = count - 1 - place if reverse else place
    gathered = jax.tree.map(lambda a: lax.all_gather(a, axis), part)
    state = jax.tree.map(lambda a, e: jnp.zeros_like(a) + jnp.asarray(e, a.dtype), part, identity)

    def one(turn, state):
        source = count - 1 - turn if reverse else turn
        return combine(
            state, jax.tree.map(lambda a: lax.dynamic_index_in_dim(a, source, 0, False), gathered)
        )

    return lax.fori_loop(0, ahead, one, state)


def compose(earlier, follower):
    early_map, early_value = earlier
    late_map, late_value = follower
    joined_map = jnp.dot(
        late_map, early_map, precision=lax.Precision.HIGHEST, preferred_element_type=jnp.float32
    )
    joined_value = (
        jnp.dot(
            late_map,
            early_value,
            precision=lax.Precision.HIGHEST,
            preferred_element_type=jnp.float32,
        )
        + late_value
    )
    return (joined_map, joined_value)


def on_device(leaf_load, leaf_map, group_map, node_index, west_coupling, east_coupling):
    exact_mode = lax.Precision.HIGHEST
    columns = leaf_load.shape[3]
    interface = group_map.shape[2]
    face_nodes = west_coupling.shape[1]
    stride = interface // face_nodes
    local_map = leaf_map[0, 0]
    local_load = leaf_load[0, 0]
    local_index = node_index[0, 0]
    contrib = jnp.dot(local_map, local_load, preferred_element_type=jnp.float32).astype(
        jnp.bfloat16
    )
    scattered = (
        jnp.zeros((interface, columns), jnp.float32)
        .at[local_index]
        .add(contrib.astype(jnp.float32))
    )
    load_share = lax.psum_scatter(
        scattered.astype(jnp.bfloat16), "grp", scatter_dimension=0, tiled=True
    )
    summed_loads = lax.all_gather(load_share, "grp", axis=0, tiled=True)
    rows_map = group_map[0]
    row_count = rows_map.shape[0]
    blocks = row_count // stride
    initial_rows = jnp.dot(rows_map, summed_loads, preferred_element_type=jnp.float32)
    block_view = rows_map.reshape(blocks, stride, face_nodes, stride)
    column_view = rows_map.reshape(row_count, face_nodes, stride)
    west_columns = column_view[:, :, 0].astype(jnp.float32)
    east_columns = column_view[:, :, 1].astype(jnp.float32)
    east_west = block_view[:, 1, :, 0].astype(jnp.float32)
    west_east = block_view[:, 0, :, 1].astype(jnp.float32)
    identity_map = jnp.eye(face_nodes, dtype=jnp.float32)
    zero_values = jnp.zeros((face_nodes, columns), jnp.float32)
    forward_maps = jnp.dot(east_west, west_coupling[0], precision=exact_mode)
    east_values = initial_rows.reshape(blocks, stride, columns)[:, 1]
    face_maps, face_values = (
        lax.all_gather(forward_maps, "grp", axis=0, tiled=True),
        lax.all_gather(east_values, "grp", axis=0, tiled=True),
    )
    _, incoming = carried_in(
        (face_maps, face_values), "dom", compose, (identity_map, zero_values), False
    )
    swept_rows = initial_rows + jnp.dot(
        west_columns,
        jnp.dot(west_coupling[0], incoming, precision=exact_mode),
        precision=exact_mode,
    )
    backward_maps = jnp.dot(west_east, east_coupling[0], precision=exact_mode)
    west_values = swept_rows.reshape(blocks, stride, columns)[:, 0]
    back_maps, back_values = (
        lax.all_gather(backward_maps, "grp", axis=0, tiled=True),
        lax.all_gather(west_values, "grp", axis=0, tiled=True),
    )
    _, outgoing = carried_in(
        (back_maps, back_values), "dom", compose, (identity_map, zero_values), True
    )
    final_rows = swept_rows + jnp.dot(
        east_columns,
        jnp.dot(east_coupling[0], outgoing, precision=exact_mode),
        precision=exact_mode,
    )
    gathered = lax.all_gather(final_rows.astype(jnp.bfloat16), "grp", axis=0, tiled=True)
    picked = gathered[local_index]
    result = lax.dot_general(
        local_map, picked, (((0,), (0,)), ((), ())), preferred_element_type=jnp.float32
    )
    result = result + local_load.astype(jnp.float32)
    return result.astype(jnp.bfloat16)[None, None]


def solution(mesh):
    return jax.shard_map(
        on_device,
        mesh=mesh,
        in_specs=(
            P("dom", "grp", None, None),
            P("dom", "grp", None, None),
            P("dom", "grp", None),
            P("dom", "grp", None),
            P("dom", None, None),
            P("dom", None, None),
        ),
        out_specs=P("dom", "grp", None, None),
        check_vma=False,
    )
```

profile of v0, /device:TPU:0, one launch (start us, length us, event | category | flops | bytes accessed | tf_op | source)
XLA Modules:
  0.0 294.7 jit_solution(9897317862429376568)
XLA Ops:
  8.1 1.6 fusion.27
  9.8 7.4 %scatter_custom_fusion = f32[4096,128]{1,0:T(8,128)} fusion(s32[1024]{0:T(1024)S(1)} %bitcast.114, f32[1024,128]{1,0:T(8,128)S(1)} %fusion.27, f32[]{:T(128)} %constant.56.clone.1), kind=kCustom, calls=%fused_computation.30 | custom fusion | flops 131072 | bytes 2097156 | tf_op jit(solution)/shard_map/scatter-add | solution.py:56
  17.2 2.7 convert_element_type.25
  20.0 29.9 %reduce-scatter.2.cloned.1.call-done = bf16[1024,128]{1,0:T(8,128)(2,1)} async-done(((bf16[4096,128]{1,0:T(8,128)(2,1)}), bf16[1024,128]{1,0:T(8,128)(2,1)}) %reduce-scatter.2.cloned.1.call-update) | async-done | bytes 262160 | tf_op jit(solution)/shard_map/reduce_scatter | solution.py:58
  50.0 62.2 %reshape_squeeze.6 = bf16[64,16,256,16]{3,2,1,0:T(8,128)(2,1)} reshape(bf16[1,1024,4096]{2,1,0:T(8,128)(2,1)} %param.12) | data formatting | bytes 16777216 | tf_op jit(solution)/shard_map/reshape;squeeze | solution.py:66
  112.1 6.2 %slice_reduce_fusion = (bf16[64,256]{1,0:T(8,128)(2,1)S(1)}, bf16[64,256]{1,0:T(8,128)(2,1)S(1)}) fusion(bf16[64,16,256,16]{3,2,1,0:T(8,128)(2,1)} %reshape_squeeze.6), kind=kLoop, calls=%fused_computation.12 | loop fusion | bytes 131072 | tf_op jit(solution)/shard_map/slice | solution.py:71
  118.6 15.0 %all_gather.43 = f32[256,256]{1,0:T(8,128)} all-gather(f32[64,256]{1,0:T(8,128)S(1)} %fusion.47), channel_id=1, replica_groups=mesh['grp'=4,'dom'=8] {'grp'}, dimensions={0}, use_global_device_ids=true | all-gather | bytes 327680 | tf_op jit(solution)/shard_map/all_gather | solution.py:77
  133.7 6.6 %fusion.15 = f32[1024,128]{0,1:T(8,128)S(1)} fusion(bf16[4096,128]{1,0:T(8,128)(2,1)} %all-gather.13.cloned.1.call-done, bf16[1,1024,4096]{2,1,0:T(8,128)(2,1)} %param.12), kind=kOutput, calls=%fused_computation.19 | convolution fusion | flops 1073741824 | bytes 9961472 | tf_op jit(solution)/shard_map/dot_general | solution.py:65
  140.3 1.0 copy.21
  142.3 14.1 %all-gather.1 = f32[256,1,128]{2,1,0:T(1,128)} all-gather(f32[64,1,128]{2,1,0:T(1,128)S(1)} %slice.27), channel_id=3, replica_groups=mesh['grp'=4,'dom'=8] {'grp'}, dimensions={0}, use_global_device_ids=true | all-gather | bytes 163840 | tf_op jit(solution)/shard_map/all_gather | solution.py:78
  156.7 14.5 %all_gather.49 = f32[256,256]{1,0:T(8,128)} all-gather(f32[64,256]{1,0:T(8,128)S(1)} %fusion.43), channel_id=1, replica_groups=mesh['grp'=4,'dom'=8] {'grp'}, dimensions={0}, use_global_device_ids=true | all-gather | bytes 327680 | tf_op jit(solution)/shard_map/all_gather | solution.py:91
  171.3 12.0 %copy.22 = bf16[1,1024,4096]{1,2,0:T(8,128)(2,1)} copy(bf16[1,1024,4096]{2,1,0:T(8,128)(2,1)} %param.12) | data formatting | bytes 16777216 | tf_op args[2]
  183.3 5.5 %fusion.49 = (bf16[1024,256,1]{0,2,1:T(2,128)(2,1)}, bf16[1024,256,1]{0,2,1:T(2,128)(2,1)}) fusion(bf16[1024,256,16]{0,2,1:T(8,128)(2,1)} %bitcast.107), kind=kLoop, calls=%fused_computation.45 | loop fusion | bytes 2097152 | tf_op jit(solution)/shard_map/slice | solution.py:69
  188.8 3.5 %copy.23 = bf16[1024,256,1]{1,0,2:T(8,128)(2,1)} copy(bf16[1024,256,1]{0,2,1:T(2,128)(2,1)} %get-tuple-element.158) | data formatting | bytes 1048576 | tf_op jit(solution)/shard_map/slice | solution.py:68
  192.7 1.7 fusion.21
  194.6 14.4 %all-gather.4 = f32[256,1,128]{2,1,0:T(1,128)} all-gather(f32[64,1,128]{2,1,0:T(1,128)S(1)} %slice.30), channel_id=6, replica_groups=mesh['grp'=4,'dom'=8] {'grp'}, dimensions={0}, use_global_device_ids=true | all-gather | bytes 163840 | tf_op jit(solution)/shard_map/all_gather | solution.py:92
  209.1 3.5 %copy.25 = bf16[1024,256,1]{1,0,2:T(8,128)(2,1)} copy(bf16[1024,256,1]{0,2,1:T(2,128)(2,1)} %get-tuple-element.157) | data formatting | bytes 1048576 | tf_op jit(solution)/shard_map/slice | solution.py:69
  212.6 2.8 all-gather.21.cloned.1.call-done
  215.3 25.4 %all-gather.23.cloned.1.call-done = f32[2048,1,128]{2,1,0:T(1,128)} async-done(((f32[256,1,128]{2,1,0:T(1,128)}), f32[2048,1,128]{2,1,0:T(1,128)}) %all-gather.23.cloned.1.call-update) | async-done | bytes 1048592 | tf_op jit(solution)/shard_map/all_gather | solution.py:11
  240.8 9.9 %while.27 = (s32[]{:T(128)}, f32[256,128]{1,0:T(8,128)S(1)}, s32[]{:T(128)}, f32[8,256,256]{2,1,0:T(8,128)}, f32[8,256,128]{2,1,0:T(8,128)}, /*index=5*/s32[]{:T(128)}, s32[]{:T(128)}, s32[]{:T(128)}, s32[]{:T(128)}) while((s32[]{:T(128)}, f32[256,128]{1,0:T(8,128)S(1)}, s32[]{:T(128)}, f32[8,256,256]{2,1,0:T(8,128)}, ...), condition=%wide.region_5.6_spmd, body=%wide.region_4.5_spmd.sunk | while | flops 100696072 | bytes 918675 | solution.py:20
  240.8 1.4 convolution_add_fusion.5
  242.2 1.4 convolution_add_fusion.5
  243.7 1.4 convolution_add_fusion.5
  245.1 1.4 convolution_add_fusion.5
  246.5 1.4 convolution_add_fusion.5
  247.9 1.4 convolution_add_fusion.5
  249.3 1.4 convolution_add_fusion.5
  251.1 2.4 fusion.23
  254.4 26.3 %all-gather.15.cloned.1.call-done = bf16[4096,128]{0,1:T(8,128)(2,1)} async-done(((bf16[1024,128]{0,1:T(8,128)(2,1)}), bf16[4096,128]{0,1:T(8,128)(2,1)}) %all-gather.15.cloned.1.call-update) | async-done | bytes 1048592 | tf_op jit(solution)/shard_map/all_gather | solution.py:102
  280.7 1.6 copy.26
  282.3 3.2 %gather_fusion = bf16[1024,128]{1,0:T(8,128)(2,1)S(1)} fusion(bf16[4096,128]{1,0:T(8,128)(2,1)S(1)} %copy.26, s32[1024]{0:T(1024)S(1)} %broadcast_clamp_fusion), kind=kCustom, calls=%fused_computation | custom fusion | bytes 528384 | tf_op jit(solution)/shard_map/gather | solution.py:103
  285.5 1.4 fusion.33
  (46 shorter events, 6.3 us)
Async XLA Ops:
  6.5 1.6 copy-start
  6.5 43.4 %reduce-scatter.2.cloned.1.call-start = ((), (), s32[]{:S(2)}) async-start(), calls=%async_computation.1 | async-start | bytes 1310720 | tf_op jit(solution)/shard_map/reduce_scatter | solution.py:58
  19.9 113.7 %all-gather.13.cloned.1.call-start = ((), (), s32[]{:S(2)}) async-start(), calls=%async_computation.2 | async-start | bytes 1310720 | tf_op jit(solution)/shard_map/all_gather | solution.py:61
  49.9 142.4 %all-gather.17.cloned.1.call-start = ((), (), s32[]{:S(2)}) async-start(), calls=%async_computation.4 | async-start | bytes 2359296 | tf_op jit(solution)/shard_map/all_gather | solution.py:11
  112.1 6.2 %copy-start.1 = (f32[1,256,256]{2,1,0:T(8,128)S(1)}, f32[1,256,256]{2,1,0:T(8,128)}, u32[]{:S(2)}) copy-start(f32[1,256,256]{2,1,0:T(8,128)} %param.14) | copy-start | bytes 786436
  133.6 22.9 %copy-start.2 = (f32[1,256,256]{2,1,0:T(8,128)S(1)}, f32[1,256,256]{2,1,0:T(8,128)}, u32[]{:S(2)}) copy-start(f32[1,256,256]{2,1,0:T(8,128)} %param.15) | copy-start | bytes 786436
  133.6 58.7 %all-gather.19.cloned.1.call-start = ((), (), s32[]{:S(2)}) async-start(), calls=%async_computation.5 | async-start | bytes 1179648 | tf_op jit(solution)/shard_map/all_gather | solution.py:11
  156.4 59.0 %all-gather.21.cloned.1.call-start = ((), (), s32[]{:S(2)}) async-start(), calls=%async_computation.6 | async-start | bytes 2359296 | tf_op jit(solution)/shard_map/all_gather | solution.py:11
  171.2 69.5 %all-gather.23.cloned.1.call-start = ((), (), s32[]{:S(2)}) async-start(), calls=%async_computation.7 | async-start | bytes 1179648 | tf_op jit(solution)/shard_map/all_gather | solution.py:11
  209.0 71.7 %all-gather.15.cloned.1.call-start = ((), (), s32[]{:S(2)}) async-start(), calls=%async_computation.3 | async-start | bytes 1310720 | tf_op jit(solution)/shard_map/all_gather | solution.py:102
  250.7 2.8 copy-start.3
Sparse Core Ops, SparseCore 0:
  20.0 29.8 reduce-scatter.1
  51.6 26.5 all-gather.12
  133.7 26.3 all-gather.16
  162.0 23.4 all-gather.18
  187.4 27.8 all-gather.20
  217.2 23.4 all-gather.22
  253.6 27.0 all-gather.14
where the time goes:
time: 297 us; the launch traced here: 295 us
  local copies, waits for them, and re-layouts  102 us (34%)
  waiting for transfers between devices  84.6 us (28%)
  blocking collectives  57.9 us (19%)
  matrix products  24.6 us (8%)
  between operations  13.7 us (5%)
  other arithmetic  10.9 us (4%)
    another operation x1, local copies, waits for them, and re-layouts, on_device(): block_view = rows_map.reshape(blocks, stride, face_nodes, stride)  62.2 us
    reduce_scatter x1, waiting for transfers between devices, on_device(): lax.psum_scatter(scattered.astype(jnp.bfloat16), 'grp', scatter_dimension...  29.9 us
    all_gather x4, waiting for transfers between devices, carried_in(): gathered = jax.tree.map(lambda a: lax.all_gather(a, axis), part)  28.2 us
    all_gather x1, waiting for transfers between devices, on_device(): lax.all_gather(final_rows.astype(jnp.bfloat16), 'grp', axis=0, tiled=True)  26.3 us
    all_gather x1, blocking collectives, on_device(): lax.all_gather(forward_maps, 'grp', axis=0, tiled=True)  15 us
    all_gather x1, blocking collectives, on_device(): lax.all_gather(backward_maps, 'grp', axis=0, tiled=True)  14.5 us
    all_gather x1, blocking collectives, on_device(): lax.all_gather(west_values, 'grp', axis=0, tiled=True)  14.4 us
    all_gather x1, blocking collectives, on_device(): lax.all_gather(east_values, 'grp', axis=0, tiled=True)  14.1 us
  transfers between devices with their start and end apart: 7, of which 4 were waited for; matrix products, arithmetic and copies ran while one was open for 36% of the time, Pallas kernels for 0%

commit v1 on v0

v1 whole, which is shorter than its diff:
```python
import functools

import jax
import jax.numpy as jnp
from jax import lax
from jax.experimental import pallas as pl
from jax.experimental.pallas import tpu as pltpu
from jax.sharding import PartitionSpec as P

MESH = pl.DeviceIdType.MESH
BF = jnp.bfloat16
F32 = jnp.float32


def dot(a, b):
    return jnp.dot(a, b, preferred_element_type=F32)


def flip(d, mask):
    out = d
    bit = 1
    while bit <= mask:
        if mask & bit:
            out = out + (1 - 2 * (lax.div(d, bit) % 2)) * bit
        bit *= 2
    return out


def subsets(bits):
    found = [0]
    for bit in bits:
        found += [m | bit for m in found]
    return found


def kernel(
    n, doms,
    lm_ref, ll_ref, g_hbm, idx_ref, wc_ref, ec_ref, out_ref,
    g, contrib, idx_all, loads, loads_b, sel, gface, gsel, maps, faces, ebuf, wbuf, swept, init, sol, pt, lmt, picked,
    g_sem, i_s, i_r, c_s, c_r, m_s, m_r, f_s, f_r, o_s, o_r, ms, mr, fs, fr_,
):
    z = lax.axis_index("grp")
    d = lax.axis_index("dom")
    rows, interface = g.shape
    nodes, cols = ll_ref.shape
    face = wc_ref.shape[0]
    stride = interface // face
    fr = rows // stride
    bits = []
    while (1 << len(bits)) < doms:
        bits.append(1 << len(bits))
    tile = 512

    load_g = pltpu.make_async_copy(g_hbm, g, g_sem)
    load_g.start()
    barrier = pltpu.get_barrier_semaphore()
    for o in range(1, n):
        pl.semaphore_signal(barrier, inc=1, device_id={"grp": (z + o) % n}, device_id_type=MESH)
    for bit in bits:
        pl.semaphore_signal(barrier, inc=1, device_id={"dom": flip(d, bit)}, device_id_type=MESH)

    contrib[z] = dot(lm_ref[...], ll_ref[...]).astype(BF)
    idx_all[z] = idx_ref[...]
    pl.semaphore_wait(barrier, n - 1 + len(bits))

    def to_group(ref, ss, rs):
        made = []
        for o in range(1, n):
            made.append(pltpu.make_async_remote_copy(
                src_ref=ref, dst_ref=ref, send_sem=ss.at[o], recv_sem=rs.at[o],
                device_id={"grp": (z + o) % n}, device_id_type=MESH))
        return made

    def start(copies):
        for c in copies:
            c.start()

    def wait(copies):
        for c in copies:
            c.wait()

    i_copies = to_group(idx_all.at[z], i_s, i_r)
    c_copies = to_group(contrib.at[z], c_s, c_r)
    start(i_copies)
    start(c_copies)

    half = interface // 2
    hf = face // 2
    a = lax.broadcasted_iota(jnp.int32, (half, face), 0)
    b = lax.broadcasted_iota(jnp.int32, (half, face), 1)
    want = jnp.where(b < hf, b * stride, (b - hf) * stride + 1)
    sel[...] = jnp.where(a == want, 1.0, 0.0).astype(BF)
    a = lax.broadcasted_iota(jnp.int32, (2 * fr, rows), 0)
    b = lax.broadcasted_iota(jnp.int32, (2 * fr, rows), 1)
    want = jnp.where(a < fr, a * stride, (a - fr) * stride + 1)
    pick_rows = jnp.where(b == want, 1.0, 0.0).astype(BF)

    load_g.wait()
    step = min(256, rows)

    @pl.loop(0, rows // step)
    def _(i):
        r0 = pl.multiple_of(i * step, step)
        for c in range(2):
            got = dot(g[pl.ds(r0, step), c * half:(c + 1) * half], sel[...]).astype(BF)
            gsel[pl.ds(r0, step), c * hf:(c + 1) * hf] = got[:, :hf]
            gsel[pl.ds(r0, step), face + c * hf:face + (c + 1) * hf] = got[:, hf:]

    ff = dot(pick_rows, gsel[...]).astype(BF)

    def split(x):
        high = x.astype(BF)
        return high, (x - high.astype(F32)).astype(BF)

    wc_h, wc_l = split(wc_ref[...])
    ec_h, ec_l = split(ec_ref[...])
    forward = dot(ff[:, :face], wc_h) + dot(ff[:, :face], wc_l)
    backward = dot(ff[:fr, face:], ec_h) + dot(ff[:fr, face:], ec_l)
    z0 = pl.multiple_of(z * fr, fr)
    maps[d, 0, pl.ds(z0, fr), :] = forward[:fr].astype(BF)
    maps[d, 1, pl.ds(z0, fr), :] = forward[fr:].astype(BF)
    maps[d, 2, pl.ds(z0, fr), :] = backward.astype(BF)
    m_copies = to_group(maps.at[d, :, pl.ds(z0, fr), :], m_s, m_r)
    start(m_copies)

    @pl.loop(0, interface // tile)
    def _(i):
        c0 = pl.multiple_of(i * tile, tile)
        gface[:, pl.ds(c0, tile)] = dot(pick_rows, g[:, pl.ds(c0, tile)]).astype(BF)

    def add_loads(block, first):
        @pl.loop(0, interface // tile)
        def _(i):
            r0 = pl.multiple_of(i * tile, tile)
            place = lax.broadcasted_iota(jnp.int32, (tile, 128), 0) + r0
            hot = jnp.concatenate([
                jnp.where(place == idx_all[block, pl.ds(r, 1), :], 1.0, 0.0).astype(BF)
                for r in range(nodes // 128)], axis=1)
            part = dot(hot, contrib[block])
            if first:
                loads[pl.ds(r0, tile), :] = part
            else:
                loads[pl.ds(r0, tile), :] += part

    def spread(ref, part, order, ss, rs):
        done, steps = [], []
        for bit in order:
            steps.append([pltpu.make_async_remote_copy(
                src_ref=ref.at[flip(d, m), part], dst_ref=ref.at[flip(d, m), part],
                send_sem=ss.at[part, m | bit], recv_sem=rs.at[part, m | bit],
                device_id={"dom": flip(d, bit)}, device_id_type=MESH) for m in subsets(done)])
            done.append(bit)
        return steps

    order_a = bits[::-1]
    order_b = order_a if len(bits) < 3 else [order_a[1], order_a[0]] + order_a[2:]
    map_steps = [spread(maps, p, (order_a, order_b, order_a)[p], ms, mr) for p in range(3)]
    face_steps = [spread(faces, p, (order_a, order_b)[p], fs, fr_) for p in range(2)]

    wait(i_copies)
    add_loads(z, True)
    wait(m_copies)
    for s in map_steps:
        start(s[0])

    turned = jnp.transpose(idx_ref[...])
    for r in range(nodes // 128):
        column = turned[:, r:r + 1]

        @pl.loop(0, interface // tile)
        def _(i):
            c0 = pl.multiple_of(i * tile, tile)
            place = lax.broadcasted_iota(jnp.int32, (128, tile), 1) + c0
            pt[r * 128:(r + 1) * 128, pl.ds(c0, tile)] = jnp.where(place == column, 1.0, 0.0).astype(BF)

    lmt[...] = jnp.transpose(lm_ref[...])

    for k in range(1, n):
        c_copies[k - 1].wait()
        add_loads((z - k + n) % n, False)
        if k < len(bits):
            for s in map_steps:
                wait(s[k - 1])
                start(s[k])
    for k in range(n, len(bits)):
        for s in map_steps:
            wait(s[k - 1])
            start(s[k])

    loads_b[...] = loads[...].astype(BF)
    here = dot(gface[...], loads_b[...]).astype(BF)
    faces[d, 0, pl.ds(z0, fr), :] = here[:fr]
    faces[d, 1, pl.ds(z0, fr), :] = here[fr:]
    f_copies = to_group(faces.at[d, :, pl.ds(z0, fr), :], f_s, f_r)
    start(f_copies)
    wait(f_copies)
    for s in face_steps:
        start(s[0])

    @pl.loop(0, rows // step)
    def _(i):
        r0 = pl.multiple_of(i * step, step)
        init[pl.ds(r0, step), :] = dot(g[pl.ds(r0, step), :], loads_b[...])

    for k in range(1, len(bits)):
        for s in face_steps:
            wait(s[k - 1])
            start(s[k])
    for s in map_steps:
        wait(s[-1])
    for s in face_steps:
        wait(s[-1])

    ebuf[0] = jnp.zeros((face, cols), BF)
    ebuf[1] = faces[0, 1]
    first = faces[0, 1].astype(F32)

    def ahead(j, carry):
        both = maps[j, pl.ds(0, 2)].reshape(2 * face, face)
        got = dot(both, ebuf[j])
        swept[j] = got[:face] + faces[j, 0].astype(F32)
        ebuf[j + 1] = (got[face:] + faces[j, 1].astype(F32)).astype(BF)
        return carry

    lax.fori_loop(1, doms, ahead, 0)
    wbuf[doms] = jnp.zeros((face, cols), BF)

    def back(t, carry):
        j = doms - 1 - t
        wbuf[j] = (swept[j] + dot(maps[j, 2], wbuf[j + 1])).astype(BF)
        return carry

    lax.fori_loop(0, doms - 1, back, 0)
    inc = ebuf[d]
    outgoing = wbuf[d + 1]
    vw = (dot(wc_h, inc) + dot(wc_l, inc)).astype(BF)
    ve = (dot(ec_h, outgoing) + dot(ec_l, outgoing)).astype(BF)
    sol[z] = (init[...] + dot(gsel[...], jnp.concatenate([vw, ve], axis=0))).astype(BF)
    o_copies = to_group(sol.at[z], o_s, o_r)
    start(o_copies)

    def add_picked(block):
        c0 = pl.multiple_of(block * rows, rows)
        return dot(pt[:, pl.ds(c0, rows)], sol[block])

    picked[...] = add_picked(z)
    for k in range(1, n):
        o_copies[k - 1].wait()
        picked[...] += add_picked((z - k + n) % n)
    out_ref[...] = (dot(lmt[...], picked[...].astype(BF)) + ll_ref[...].astype(F32)).astype(BF)


def solution(mesh):
    n, doms = mesh.shape["grp"], mesh.shape["dom"]

    def on_device(leaf_load, leaf_map, group_map, node_index, west_coupling, east_coupling):
        nodes, cols = leaf_load.shape[2:]
        rows, interface = group_map.shape[1:]
        face = west_coupling.shape[1]
        fr = rows // (interface // face)
        vm = pl.BlockSpec(memory_space=pltpu.VMEM)
        dma = pltpu.SemaphoreType.DMA
        out = pl.pallas_call(
            functools.partial(kernel, n, doms),
            out_shape=jax.ShapeDtypeStruct((nodes, cols), BF),
            in_specs=[vm, vm, pl.BlockSpec(memory_space=pl.ANY), vm, vm, vm],
            out_specs=vm,
            scratch_shapes=[
                pltpu.VMEM((rows, interface), BF),
                pltpu.VMEM((n, nodes, cols), BF),
                pltpu.VMEM((n, nodes // 128, 128), jnp.int32),
                pltpu.VMEM((interface, cols), F32),
                pltpu.VMEM((interface, cols), BF),
                pltpu.VMEM((interface // 2, face), BF),
                pltpu.VMEM((2 * fr, interface), BF),
                pltpu.VMEM((rows, 2 * face), BF),
                pltpu.VMEM((doms, 3, face, face), BF),
                pltpu.VMEM((doms, 2, face, cols), BF),
                pltpu.VMEM((doms + 1, face, cols), BF),
                pltpu.VMEM((doms + 1, face, cols), BF),
                pltpu.VMEM((doms, face, cols), F32),
                pltpu.VMEM((rows, cols), F32),
                pltpu.VMEM((n, rows, cols), BF),
                pltpu.VMEM((nodes, interface), BF),
                pltpu.VMEM((nodes, nodes), BF),
                pltpu.VMEM((nodes, cols), F32),
                dma, dma((n,)), dma((n,)), dma((n,)), dma((n,)), dma((n,)), dma((n,)),
                dma((n,)), dma((n,)), dma((n,)), dma((n,)),
                dma((3, doms)), dma((3, doms)), dma((2, doms)), dma((2, doms)),
            ],
            compiler_params=pltpu.CompilerParams(
                collective_id=0, has_side_effects=True, vmem_limit_bytes=60 * 1024 * 1024
            ),
            cost_estimate=pl.CostEstimate(flops=10**10, bytes_accessed=11 * 10**6, transcendentals=0),
        )(
            leaf_map[0, 0], leaf_load[0, 0], group_map[0], node_index.reshape(nodes // 128, 128),
            west_coupling[0], east_coupling[0],
        )
        return out[None, None]

    return jax.shard_map(
        on_device,
        mesh=mesh,
        in_specs=(
            P("dom", "grp", None, None),
            P("dom", "grp", None, None),
            P("dom", "grp", None),
            P("dom", "grp", None),
            P("dom", None, None),
            P("dom", None, None),
        ),
        out_specs=P("dom", "grp", None, None),
        check_vma=False,
    )
```

time: 297 us -> 112 us (0.38)
  the two profiles are of different devices: /device:TPU:0 before, /device:TPU:24 now
where the time goes in v1:
time: 112 us
  Pallas kernels  110 us (98%)
  local copies, waits for them, and re-layouts  1.67 us (1%)
    pallas_call x1, Pallas kernels, on_device(): pl.pallas_call(functools.partial(kernel, n, doms), out_shape=jax.ShapeDty...  110 us

profile of v1, /device:TPU:24, one launch (start us, length us, event | category | flops | bytes accessed | tf_op | source)
XLA Modules:
  0.0 111.7 jit_solution(16500053329308062616)
XLA Ops:
  0.0 110.0 %shard_map.64 = bf16[1024,128]{1,0:T(8,128)(2,1)} custom-call(bf16[1024,1024]{1,0:T(8,128)(2,1)} %bitcast.9, bf16[1024,128]{1,0:T(8,128)(2,1)} %bitcast.10, bf16[1024,4096]{1,0:T(8,128)(2,1)} %bitcast.8, s32[8,128]{1,0:T(8,128)} %bitcast.13, f32[256,256]{1,0:T(8,128)} %bitcast.11, f32[256,256]{1,0:T(8,128)} %bitcast.12), custom_call_target="tpu_custom_call" | custom-call | flops 10000000000 | bytes 11000000 | tf_op jit(solution)/shard_map/pallas_call | solution.py:263
  110.1 1.7 %copy.8 = bf16[1,1,1024,128]{3,2,1,0:T(8,128)(2,1)} copy(bf16[1,1,1024,128]{3,2,1,0:T(8,128)(2,1)} %bitcast.7) | data formatting | bytes 524288

commit v2 on v1

--- a/solution.py
+++ b/solution.py
@@ -36,7 +36,7 @@
 def kernel(
     n, doms,
     lm_ref, ll_ref, g_hbm, idx_ref, wc_ref, ec_ref, out_ref,
-    g, contrib, idx_all, loads, loads_b, sel, gface, gsel, maps, faces, ebuf, wbuf, swept, init, sol, pt, lmt, picked,
+    g, contrib, idx_all, loads, loads_b, sel, gface, gsel, maps, faces, ebuf, wbuf, swept, init, sol, pt, lmt, picked, plast,
     g_sem, i_s, i_r, c_s, c_r, m_s, m_r, f_s, f_r, o_s, o_r, ms, mr, fs, fr_,
 ):
     z = lax.axis_index("grp")
@@ -128,15 +128,17 @@
         c0 = pl.multiple_of(i * tile, tile)
         gface[:, pl.ds(c0, tile)] = dot(pick_rows, g[:, pl.ds(c0, tile)]).astype(BF)
 
+    def one_hot(block, r0):
+        place = lax.broadcasted_iota(jnp.int32, (tile, 128), 0) + r0
+        return jnp.concatenate([
+            jnp.where(place == idx_all[block, pl.ds(r, 1), :], 1.0, 0.0).astype(BF)
+            for r in range(nodes // 128)], axis=1)
+
     def add_loads(block, first):
         @pl.loop(0, interface // tile)
         def _(i):
             r0 = pl.multiple_of(i * tile, tile)
-            place = lax.broadcasted_iota(jnp.int32, (tile, 128), 0) + r0
-            hot = jnp.concatenate([
-                jnp.where(place == idx_all[block, pl.ds(r, 1), :], 1.0, 0.0).astype(BF)
-                for r in range(nodes // 128)], axis=1)
-            part = dot(hot, contrib[block])
+            part = dot(one_hot(block, r0), contrib[block])
             if first:
                 loads[pl.ds(r0, tile), :] = part
             else:
@@ -175,24 +177,42 @@
 
     lmt[...] = jnp.transpose(lm_ref[...])
 
-    for k in range(1, n):
+    last = (z + 1) % n
+    gp = jnp.zeros((2 * fr, nodes), F32)
+
+    def prepare(i, gp):
+        r0 = pl.multiple_of(i * tile, tile)
+        hot = one_hot(last, r0)
+        plast[pl.ds(r0, tile), :] = hot
+        return gp + dot(gface[:, pl.ds(r0, tile)], hot)
+
+    gp = lax.fori_loop(0, interface // tile, prepare, gp).astype(BF)
+
+    for k in range(1, n - 1):
         c_copies[k - 1].wait()
         add_loads((z - k + n) % n, False)
         if k < len(bits):
             for s in map_steps:
                 wait(s[k - 1])
                 start(s[k])
-    for k in range(n, len(bits)):
+    for k in range(n - 1, len(bits)):
         for s in map_steps:
             wait(s[k - 1])
             start(s[k])
 
-    loads_b[...] = loads[...].astype(BF)
-    here = dot(gface[...], loads_b[...]).astype(BF)
+    here = dot(gface[...], loads[...].astype(BF))
+    c_copies[n - 2].wait()
+    here = (here + dot(gp, contrib[last])).astype(BF)
     faces[d, 0, pl.ds(z0, fr), :] = here[:fr]
     faces[d, 1, pl.ds(z0, fr), :] = here[fr:]
     f_copies = to_group(faces.at[d, :, pl.ds(z0, fr), :], f_s, f_r)
     start(f_copies)
+
+    @pl.loop(0, interface // tile)
+    def _(i):
+        r0 = pl.multiple_of(i * tile, tile)
+        loads_b[pl.ds(r0, tile), :] = (loads[pl.ds(r0, tile), :] + dot(plast[pl.ds(r0, tile), :], contrib[last])).astype(BF)
+
     wait(f_copies)
     for s in face_steps:
         start(s[0])
@@ -222,7 +242,7 @@
         ebuf[j + 1] = (got[face:] + faces[j, 1].astype(F32)).astype(BF)
         return carry
 
-    lax.fori_loop(1, doms, ahead, 0)
+    lax.fori_loop(1, doms, ahead, 0, unroll=True)
     wbuf[doms] = jnp.zeros((face, cols), BF)
 
     def back(t, carry):
@@ -230,23 +250,61 @@
         wbuf[j] = (swept[j] + dot(maps[j, 2], wbuf[j + 1])).astype(BF)
         return carry
 
-    lax.fori_loop(0, doms - 1, back, 0)
+    lax.fori_loop(0, doms - 1, back, 0, unroll=True)
     inc = ebuf[d]
     outgoing = wbuf[d + 1]
     vw = (dot(wc_h, inc) + dot(wc_l, inc)).astype(BF)
     ve = (dot(ec_h, outgoing) + dot(ec_l, outgoing)).astype(BF)
     sol[z] = (init[...] + dot(gsel[...], jnp.concatenate([vw, ve], axis=0))).astype(BF)
-    o_copies = to_group(sol.at[z], o_s, o_r)
-    start(o_copies)
+    chunks = o_r.shape[1]
+    span = rows // chunks
+
+    def passing(block, c, way):
+        ref = sol.at[block, pl.ds(c * span, span), :]
+        return pltpu.make_async_remote_copy(
+            src_ref=ref, dst_ref=ref, send_sem=o_s.at[way, block, c], recv_sem=o_r.at[block, c],
+            device_id={"grp": z + 1 - 2 * way}, device_id_type=MESH)
 
     def add_picked(block):
         c0 = pl.multiple_of(block * rows, rows)
         return dot(pt[:, pl.ds(c0, rows)], sol[block])
 
-    picked[...] = add_picked(z)
-    for k in range(1, n):
-        o_copies[k - 1].wait()
-        picked[...] += add_picked((z - k + n) % n)
+    can = (z < n - 1, z > 0)
+
+    def have(s, way):
+        return z >= s if way == 0 else z + s < n
+
+    for s in range(n):
+        for c in range(chunks):
+            for way in range(2):
+                block = z - s if way == 0 else z + s
+                if s:
+                    @pl.when(have(s, way))
+                    def _():
+                        passing(block, c, way).wait_recv()
+
+                @pl.when(jnp.logical_and(have(s, way), can[way]))
+                def _():
+                    passing(block, c, way).start()
+        if s == 0:
+            picked[...] = add_picked(z)
+            continue
+        for way in range(2):
+            block = z - s if way == 0 else z + s
+
+            @pl.when(have(s, way))
+            def _():
+                picked[...] += add_picked(block)
+
+    for s in range(n - 1):
+        for c in range(chunks):
+            for way in range(2):
+                block = z - s if way == 0 else z + s
+
+                @pl.when(jnp.logical_and(have(s, way), can[way]))
+                def _():
+                    passing(block, c, way).wait_send()
+
     out_ref[...] = (dot(lmt[...], picked[...].astype(BF)) + ll_ref[...].astype(F32)).astype(BF)
 
 
@@ -284,8 +342,9 @@
                 pltpu.VMEM((nodes, interface), BF),
                 pltpu.VMEM((nodes, nodes), BF),
                 pltpu.VMEM((nodes, cols), F32),
+                pltpu.VMEM((interface, nodes), BF),
                 dma, dma((n,)), dma((n,)), dma((n,)), dma((n,)), dma((n,)), dma((n,)),
-                dma((n,)), dma((n,)), dma((n,)), dma((n,)),
+                dma((n,)), dma((n,)), dma((2, n, 4)), dma((n, 4)),
                 dma((3, doms)), dma((3, doms)), dma((2, doms)), dma((2, doms)),
             ],
             compiler_params=pltpu.CompilerParams(

time: 112 us -> 107 us (0.955)
  the two profiles are of different devices: /device:TPU:24 before, /device:TPU:0 now
where the time goes in v2:
time: 107 us
  Pallas kernels  105 us (98%)
  local copies, waits for them, and re-layouts  1.67 us (2%)
    pallas_call x1, Pallas kernels, on_device(): pl.pallas_call(functools.partial(kernel, n, doms), out_shape=jax.ShapeDty...  105 us

profile of v2, /device:TPU:0, one launch (start us, length us, event | category | flops | bytes accessed | tf_op | source)
XLA Modules:
  0.0 107.0 jit_solution(4393107879330014910)
XLA Ops:
  0.0 105.3 %shard_map.64 = bf16[1024,128]{1,0:T(8,128)(2,1)} custom-call(bf16[1024,1024]{1,0:T(8,128)(2,1)} %bitcast.9, bf16[1024,128]{1,0:T(8,128)(2,1)} %bitcast.10, bf16[1024,4096]{1,0:T(8,128)(2,1)} %bitcast.8, s32[8,128]{1,0:T(8,128)} %bitcast.13, f32[256,256]{1,0:T(8,128)} %bitcast.11, f32[256,256]{1,0:T(8,128)} %bitcast.12), custom_call_target="tpu_custom_call" | custom-call | flops 10000000000 | bytes 11000000 | tf_op jit(solution)/shard_map/pallas_call | solution.py:321
  105.4 1.7 %copy.8 = bf16[1,1,1024,128]{3,2,1,0:T(8,128)(2,1)} copy(bf16[1,1,1024,128]{3,2,1,0:T(8,128)(2,1)} %bitcast.7) | data formatting | bytes 524288

commit v3 on v2

--- a/solution.py
+++ b/solution.py
@@ -75,14 +75,16 @@
         for c in copies:
             c.start()
 
+    sent = []
+
     def wait(copies):
         for c in copies:
-            c.wait()
+            c.wait_recv()
+        sent.extend(copies)
 
     i_copies = to_group(idx_all.at[z], i_s, i_r)
     c_copies = to_group(contrib.at[z], c_s, c_r)
     start(i_copies)
-    start(c_copies)
 
     half = interface // 2
     hf = face // 2
@@ -96,17 +98,13 @@
     pick_rows = jnp.where(b == want, 1.0, 0.0).astype(BF)
 
     load_g.wait()
-    step = min(256, rows)
-
-    @pl.loop(0, rows // step)
+    @pl.loop(0, interface // tile)
     def _(i):
-        r0 = pl.multiple_of(i * step, step)
-        for c in range(2):
-            got = dot(g[pl.ds(r0, step), c * half:(c + 1) * half], sel[...]).astype(BF)
-            gsel[pl.ds(r0, step), c * hf:(c + 1) * hf] = got[:, :hf]
-            gsel[pl.ds(r0, step), face + c * hf:face + (c + 1) * hf] = got[:, hf:]
-
-    ff = dot(pick_rows, gsel[...]).astype(BF)
+        c0 = pl.multiple_of(i * tile, tile)
+        gface[:, pl.ds(c0, tile)] = dot(pick_rows, g[:, pl.ds(c0, tile)]).astype(BF)
+
+    got = [dot(gface[:, c * half:(c + 1) * half], sel[...]).astype(BF) for c in range(2)]
+    ff = jnp.concatenate([got[0][:, :hf], got[1][:, :hf], got[0][:, hf:], got[1][:, hf:]], axis=1)
 
     def split(x):
         high = x.astype(BF)
@@ -123,16 +121,36 @@
     m_copies = to_group(maps.at[d, :, pl.ds(z0, fr), :], m_s, m_r)
     start(m_copies)
 
-    @pl.loop(0, interface // tile)
+    start(c_copies)
+
+    step = min(256, rows)
+
+    @pl.loop(0, rows // step)
     def _(i):
-        c0 = pl.multiple_of(i * tile, tile)
-        gface[:, pl.ds(c0, tile)] = dot(pick_rows, g[:, pl.ds(c0, tile)]).astype(BF)
+        r0 = pl.multiple_of(i * step, step)
+        for c in range(2):
+            got = dot(g[pl.ds(r0, step), c * half:(c + 1) * half], sel[...]).astype(BF)
+            gsel[pl.ds(r0, step), c * hf:(c + 1) * hf] = got[:, :hf]
+            gsel[pl.ds(r0, step), face + c * hf:face + (c + 1) * hf] = got[:, hf:]
 
     def one_hot(block, r0):
         place = lax.broadcasted_iota(jnp.int32, (tile, 128), 0) + r0
         return jnp.concatenate([
             jnp.where(place == idx_all[block, pl.ds(r, 1), :], 1.0, 0.0).astype(BF)
             for r in range(nodes // 128)], axis=1)
+
+    upper = 2 * z < n
+    near = jnp.where(upper, z, n - 1 - z)
+
+    def arrival(t):
+        far = jnp.where(upper, z + (t - near + 1), z - (t - near + 1))
+        return jnp.where(t < 2 * near, z + (t // 2 + 1) * (1 - t % 2 * 2), far)
+
+    def take(block):
+        o = (z - block + n) % n
+        pltpu.make_async_remote_copy(
+            src_ref=contrib.at[block], dst_ref=contrib.at[block], send_sem=c_s.at[o], recv_sem=c_r.at[o],
+            device_id={"grp": block}, device_id_type=MESH).wait_recv()
 
     def add_loads(block, first):
         @pl.loop(0, interface // tile)
@@ -144,11 +162,11 @@
             else:
                 loads[pl.ds(r0, tile), :] += part
 
-    def spread(ref, part, order, ss, rs):
+    def spread(ref, part, order, ss, rs, pick):
         done, steps = [], []
         for bit in order:
             steps.append([pltpu.make_async_remote_copy(
-                src_ref=ref.at[flip(d, m), part], dst_ref=ref.at[flip(d, m), part],
+                src_ref=ref.at[flip(d, m), *pick], dst_ref=ref.at[flip(d, m), *pick],
                 send_sem=ss.at[part, m | bit], recv_sem=rs.at[part, m | bit],
                 device_id={"dom": flip(d, bit)}, device_id_type=MESH) for m in subsets(done)])
             done.append(bit)
@@ -156,8 +174,9 @@
 
     order_a = bits[::-1]
     order_b = order_a if len(bits) < 3 else [order_a[1], order_a[0]] + order_a[2:]
-    map_steps = [spread(maps, p, (order_a, order_b, order_a)[p], ms, mr) for p in range(3)]
-    face_steps = [spread(faces, p, (order_a, order_b)[p], fs, fr_) for p in range(2)]
+    map_steps = [
+        spread(maps, p, (order_a, order_b)[p % 2], ms, mr, (p // 2, pl.ds(p % 2 * hf, hf))) for p in range(6)]
+    face_steps = [spread(faces, p, (order_a, order_b)[p], fs, fr_, (p,)) for p in range(2)]
 
     wait(i_copies)
     add_loads(z, True)
@@ -177,7 +196,12 @@
 
     lmt[...] = jnp.transpose(lm_ref[...])
 
-    last = (z + 1) % n
+    if len(bits) > 1:
+        for s in map_steps:
+            wait(s[0])
+            start(s[1])
+
+    last = arrival(n - 2)
     gp = jnp.zeros((2 * fr, nodes), F32)
 
     def prepare(i, gp):
@@ -188,20 +212,18 @@
 
     gp = lax.fori_loop(0, interface // tile, prepare, gp).astype(BF)
 
-    for k in range(1, n - 1):
-        c_copies[k - 1].wait()
-        add_loads((z - k + n) % n, False)
-        if k < len(bits):
-            for s in map_steps:
-                wait(s[k - 1])
-                start(s[k])
-    for k in range(n - 1, len(bits)):
+    for t in range(n - 2):
+        block = arrival(t)
+        take(block)
+        add_loads(block, False)
+    for k in range(2, len(bits)):
         for s in map_steps:
             wait(s[k - 1])
             start(s[k])
 
     here = dot(gface[...], loads[...].astype(BF))
-    c_copies[n - 2].wait()
+    take(last)
+    sent.extend(c_copies)
     here = (here + dot(gp, contrib[last])).astype(BF)
     faces[d, 0, pl.ds(z0, fr), :] = here[:fr]
     faces[d, 1, pl.ds(z0, fr), :] = here[fr:]
@@ -233,7 +255,6 @@
 
     ebuf[0] = jnp.zeros((face, cols), BF)
     ebuf[1] = faces[0, 1]
-    first = faces[0, 1].astype(F32)
 
     def ahead(j, carry):
         both = maps[j, pl.ds(0, 2)].reshape(2 * face, face)
@@ -296,6 +317,8 @@
             def _():
                 picked[...] += add_picked(block)
 
+    for c in sent:
+        c.wait_send()
     for s in range(n - 1):
         for c in range(chunks):
             for way in range(2):
@@ -345,7 +368,7 @@
                 pltpu.VMEM((interface, nodes), BF),
                 dma, dma((n,)), dma((n,)), dma((n,)), dma((n,)), dma((n,)), dma((n,)),
                 dma((n,)), dma((n,)), dma((2, n, 4)), dma((n, 4)),
-                dma((3, doms)), dma((3, doms)), dma((2, doms)), dma((2, doms)),
+                dma((6, doms)), dma((6, doms)), dma((2, doms)), dma((2, doms)),
             ],
             compiler_params=pltpu.CompilerParams(
                 collective_id=0, has_side_effects=True, vmem_limit_bytes=60 * 1024 * 1024

time: 107 us -> 91.8 us (0.86)
  Pallas kernels: 105 us -> 89.4 us
    pallas_call x1, Pallas kernels: 105 us -> 89.4 us  [on_device(): pl.pallas_call(functools.partial(kernel, n, doms), out_shape=jax.ShapeDty...]
where the time goes in v3:
time: 91.8 us; the launch traced here: 91.1 us
  Pallas kernels  89.4 us (97%)
  local copies, waits for them, and re-layouts  1.67 us (2%)
    pallas_call x1, Pallas kernels, on_device(): pl.pallas_call(functools.partial(kernel, n, doms), out_shape=jax.ShapeDty...  89.4 us

profile of v3, /device:TPU:0, one launch (start us, length us, event | category | flops | bytes accessed | tf_op | source)
XLA Modules:
  0.0 91.1 jit_solution(8812020293244894717)
XLA Ops:
  0.0 89.4 %shard_map.64 = bf16[1024,128]{1,0:T(8,128)(2,1)} custom-call(bf16[1024,1024]{1,0:T(8,128)(2,1)} %bitcast.9, bf16[1024,128]{1,0:T(8,128)(2,1)} %bitcast.10, bf16[1024,4096]{1,0:T(8,128)(2,1)} %bitcast.8, s32[8,128]{1,0:T(8,128)} %bitcast.13, f32[256,256]{1,0:T(8,128)} %bitcast.11, f32[256,256]{1,0:T(8,128)} %bitcast.12), custom_call_target="tpu_custom_call" | custom-call | flops 10000000000 | bytes 11000000 | tf_op jit(solution)/shard_map/pallas_call | solution.py:344
  89.4 1.7 %copy.8 = bf16[1,1,1024,128]{3,2,1,0:T(8,128)(2,1)} copy(bf16[1,1,1024,128]{3,2,1,0:T(8,128)(2,1)} %bitcast.7) | data formatting | bytes 524288

commit v4 on v3

--- a/solution.py
+++ b/solution.py
@@ -123,21 +123,15 @@
 
     start(c_copies)
 
-    step = min(256, rows)
-
-    @pl.loop(0, rows // step)
-    def _(i):
-        r0 = pl.multiple_of(i * step, step)
-        for c in range(2):
-            got = dot(g[pl.ds(r0, step), c * half:(c + 1) * half], sel[...]).astype(BF)
-            gsel[pl.ds(r0, step), c * hf:(c + 1) * hf] = got[:, :hf]
-            gsel[pl.ds(r0, step), face + c * hf:face + (c + 1) * hf] = got[:, hf:]
+    place = lax.broadcasted_iota(jnp.int32, (tile, 128), 0).astype(jnp.int16)
 
     def one_hot(block, r0):
-        place = lax.broadcasted_iota(jnp.int32, (tile, 128), 0) + r0
-        return jnp.concatenate([
-            jnp.where(place == idx_all[block, pl.ds(r, 1), :], 1.0, 0.0).astype(BF)
-            for r in range(nodes // 128)], axis=1)
+        made = []
+        for r in range(nodes // 128):
+            row = jnp.broadcast_to(idx_all[block, pl.ds(r, 1), :] - r0, (16, 128)).astype(jnp.int16)
+            row = jnp.concatenate([row] * (tile // 16), axis=0)
+            made.append(jnp.where(place == row, jnp.ones((), BF), jnp.zeros((), BF)))
+        return jnp.concatenate(made, axis=1)
 
     upper = 2 * z < n
     near = jnp.where(upper, z, n - 1 - z)
@@ -184,23 +178,6 @@
     for s in map_steps:
         start(s[0])
 
-    turned = jnp.transpose(idx_ref[...])
-    for r in range(nodes // 128):
-        column = turned[:, r:r + 1]
-
-        @pl.loop(0, interface // tile)
-        def _(i):
-            c0 = pl.multiple_of(i * tile, tile)
-            place = lax.broadcasted_iota(jnp.int32, (128, tile), 1) + c0
-            pt[r * 128:(r + 1) * 128, pl.ds(c0, tile)] = jnp.where(place == column, 1.0, 0.0).astype(BF)
-
-    lmt[...] = jnp.transpose(lm_ref[...])
-
-    if len(bits) > 1:
-        for s in map_steps:
-            wait(s[0])
-            start(s[1])
-
     last = arrival(n - 2)
     gp = jnp.zeros((2 * fr, nodes), F32)
 
@@ -211,6 +188,11 @@
         return gp + dot(gface[:, pl.ds(r0, tile)], hot)
 
     gp = lax.fori_loop(0, interface // tile, prepare, gp).astype(BF)
+
+    if len(bits) > 1:
+        for s in map_steps:
+            wait(s[0])
+            start(s[1])
 
     for t in range(n - 2):
         block = arrival(t)
@@ -239,39 +221,54 @@
     for s in face_steps:
         start(s[0])
 
-    @pl.loop(0, rows // step)
-    def _(i):
-        r0 = pl.multiple_of(i * step, step)
-        init[pl.ds(r0, step), :] = dot(g[pl.ds(r0, step), :], loads_b[...])
-
+    step = min(256, rows)
+
+    def take_columns():
+        @pl.loop(0, rows // step)
+        def _(i):
+            r0 = pl.multiple_of(i * step, step)
+            for c in range(2):
+                got = dot(g[pl.ds(r0, step), c * half:(c + 1) * half], sel[...]).astype(BF)
+                gsel[pl.ds(r0, step), c * hf:(c + 1) * hf] = got[:, :hf]
+                gsel[pl.ds(r0, step), face + c * hf:face + (c + 1) * hf] = got[:, hf:]
+
+    def start_rows():
+        @pl.loop(0, rows // step)
+        def _(i):
+            r0 = pl.multiple_of(i * step, step)
+            init[pl.ds(r0, step), :] = dot(g[pl.ds(r0, step), :], loads_b[...])
+
+    def turn_map():
+        lmt[...] = jnp.transpose(lm_ref[...])
+
+    beside = [take_columns, start_rows, turn_map]
     for k in range(1, len(bits)):
+        if beside:
+            beside.pop(0)()
         for s in face_steps:
             wait(s[k - 1])
             start(s[k])
+    for work in beside:
+        work()
     for s in map_steps:
         wait(s[-1])
     for s in face_steps:
         wait(s[-1])
 
     ebuf[0] = jnp.zeros((face, cols), BF)
-    ebuf[1] = faces[0, 1]
-
-    def ahead(j, carry):
-        both = maps[j, pl.ds(0, 2)].reshape(2 * face, face)
-        got = dot(both, ebuf[j])
-        swept[j] = got[:face] + faces[j, 0].astype(F32)
-        ebuf[j + 1] = (got[face:] + faces[j, 1].astype(F32)).astype(BF)
-        return carry
-
-    lax.fori_loop(1, doms, ahead, 0, unroll=True)
+    east = faces[0, 1]
+    ebuf[1] = east
+    for j in range(1, doms):
+        swept[j] = dot(maps[j, 0], east) + faces[j, 0].astype(F32)
+        if j < doms - 1:
+            east = (dot(maps[j, 1], east) + faces[j, 1].astype(F32)).astype(BF)
+            ebuf[j + 1] = east
     wbuf[doms] = jnp.zeros((face, cols), BF)
-
-    def back(t, carry):
-        j = doms - 1 - t
-        wbuf[j] = (swept[j] + dot(maps[j, 2], wbuf[j + 1])).astype(BF)
-        return carry
-
-    lax.fori_loop(0, doms - 1, back, 0, unroll=True)
+    west = swept[doms - 1].astype(BF)
+    wbuf[doms - 1] = west
+    for j in range(doms - 2, 0, -1):
+        west = (swept[j] + dot(maps[j, 2], west)).astype(BF)
+        wbuf[j] = west
     inc = ebuf[d]
     outgoing = wbuf[d + 1]
     vw = (dot(wc_h, inc) + dot(wc_l, inc)).astype(BF)
@@ -285,6 +282,17 @@
         return pltpu.make_async_remote_copy(
             src_ref=ref, dst_ref=ref, send_sem=o_s.at[way, block, c], recv_sem=o_r.at[block, c],
             device_id={"grp": z + 1 - 2 * way}, device_id_type=MESH)
+
+    def turn_index():
+        turned = jnp.transpose(idx_ref[...])
+        for r in range(nodes // 128):
+            column = turned[:, r:r + 1]
+
+            @pl.loop(0, interface // tile)
+            def _(i):
+                c0 = pl.multiple_of(i * tile, tile)
+                place = lax.broadcasted_iota(jnp.int32, (128, tile), 1) + c0
+                pt[r * 128:(r + 1) * 128, pl.ds(c0, tile)] = jnp.where(place == column, 1.0, 0.0).astype(BF)
 
     def add_picked(block):
         c0 = pl.multiple_of(block * rows, rows)
@@ -308,6 +316,7 @@
                 def _():
                     passing(block, c, way).start()
         if s == 0:
+            turn_index()
             picked[...] = add_picked(z)
             continue
         for way in range(2):

time: 91.8 us -> 93.2 us (1.015)
  Pallas kernels: 89.4 us -> 91.4 us
    pallas_call x1, Pallas kernels: 89.4 us -> 91.4 us  [on_device(): pl.pallas_call(functools.partial(kernel, n, doms), out_shape=jax.ShapeDty...]
where the time goes in v4:
time: 93.2 us; the launch traced here: 93 us
  Pallas kernels  91.4 us (98%)
  local copies, waits for them, and re-layouts  1.67 us (2%)
    pallas_call x1, Pallas kernels, on_device(): pl.pallas_call(functools.partial(kernel, n, doms), out_shape=jax.ShapeDty...  91.4 us

profile of v4, /device:TPU:0, one launch (start us, length us, event | category | flops | bytes accessed | tf_op | source)
XLA Modules:
  0.0 93.0 jit_solution(10145179233549367678)
XLA Ops:
  0.0 91.4 %shard_map.64 = bf16[1024,128]{1,0:T(8,128)(2,1)} custom-call(bf16[1024,1024]{1,0:T(8,128)(2,1)} %bitcast.9, bf16[1024,128]{1,0:T(8,128)(2,1)} %bitcast.10, bf16[1024,4096]{1,0:T(8,128)(2,1)} %bitcast.8, s32[8,128]{1,0:T(8,128)} %bitcast.13, f32[256,256]{1,0:T(8,128)} %bitcast.11, f32[256,256]{1,0:T(8,128)} %bitcast.12), custom_call_target="tpu_custom_call" | custom-call | flops 10000000000 | bytes 11000000 | tf_op jit(solution)/shard_map/pallas_call | solution.py:353
  91.4 1.7 %copy.8 = bf16[1,1,1024,128]{3,2,1,0:T(8,128)(2,1)} copy(bf16[1,1,1024,128]{3,2,1,0:T(8,128)(2,1)} %bitcast.7) | data formatting | bytes 524288

commit v5 on v4

--- a/solution.py
+++ b/solution.py
@@ -82,8 +82,49 @@
             c.wait_recv()
         sent.extend(copies)
 
+    can = (z < n - 1, z > 0)
+
+    def have(s, way):
+        return z >= s if way == 0 else z + s < n
+
+    def line(buf, ss, rs):
+        chunks = rs.shape[1]
+        span = buf.shape[1] // chunks
+
+        def passing(block, c, way):
+            ref = buf.at[block, pl.ds(c * span, span), :]
+            return pltpu.make_async_remote_copy(
+                src_ref=ref, dst_ref=ref, send_sem=ss.at[way, block, c], recv_sem=rs.at[block, c],
+                device_id={"grp": z + 1 - 2 * way}, device_id_type=MESH)
+
+        def move(s):
+            for c in range(chunks):
+                for way in range(2):
+                    block = z - s if way == 0 else z + s
+                    if s:
+                        @pl.when(have(s, way))
+                        def _():
+                            passing(block, c, way).wait_recv()
+
+                    @pl.when(jnp.logical_and(have(s, way), can[way]))
+                    def _():
+                        passing(block, c, way).start()
+
+        def end():
+            for s in range(n - 1):
+                for c in range(chunks):
+                    for way in range(2):
+                        block = z - s if way == 0 else z + s
+
+                        @pl.when(jnp.logical_and(have(s, way), can[way]))
+                        def _():
+                            passing(block, c, way).wait_send()
+
+        return move, end
+
+    move_contrib, end_contrib = line(contrib, c_s, c_r)
+    move_sol, end_sol = line(sol, o_s, o_r)
     i_copies = to_group(idx_all.at[z], i_s, i_r)
-    c_copies = to_group(contrib.at[z], c_s, c_r)
     start(i_copies)
 
     half = interface // 2
@@ -121,7 +162,7 @@
     m_copies = to_group(maps.at[d, :, pl.ds(z0, fr), :], m_s, m_r)
     start(m_copies)
 
-    start(c_copies)
+    move_contrib(0)
 
     place = lax.broadcasted_iota(jnp.int32, (tile, 128), 0).astype(jnp.int16)
 
@@ -139,12 +180,6 @@
     def arrival(t):
         far = jnp.where(upper, z + (t - near + 1), z - (t - near + 1))
         return jnp.where(t < 2 * near, z + (t // 2 + 1) * (1 - t % 2 * 2), far)
-
-    def take(block):
-        o = (z - block + n) % n
-        pltpu.make_async_remote_copy(
-            src_ref=contrib.at[block], dst_ref=contrib.at[block], send_sem=c_s.at[o], recv_sem=c_r.at[o],
-            device_id={"grp": block}, device_id_type=MESH).wait_recv()
 
     def add_loads(block, first):
         @pl.loop(0, interface // tile)
@@ -172,8 +207,20 @@
         spread(maps, p, (order_a, order_b)[p % 2], ms, mr, (p // 2, pl.ds(p % 2 * hf, hf))) for p in range(6)]
     face_steps = [spread(faces, p, (order_a, order_b)[p], fs, fr_, (p,)) for p in range(2)]
 
+    def turn_index():
+        turned = jnp.transpose(idx_ref[...])
+        for r in range(nodes // 128):
+            column = turned[:, r:r + 1]
+
+            @pl.loop(0, interface // tile)
+            def _(i):
+                c0 = pl.multiple_of(i * tile, tile)
+                place = lax.broadcasted_iota(jnp.int32, (128, tile), 1) + c0
+                pt[r * 128:(r + 1) * 128, pl.ds(c0, tile)] = jnp.where(place == column, 1.0, 0.0).astype(BF)
+
     wait(i_copies)
     add_loads(z, True)
+    turn_index()
     wait(m_copies)
     for s in map_steps:
         start(s[0])
@@ -195,17 +242,19 @@
             start(s[1])
 
     for t in range(n - 2):
-        block = arrival(t)
-        take(block)
-        add_loads(block, False)
-    for k in range(2, len(bits)):
+        move_contrib(t + 1)
+        if 1 <= t < len(bits) - 1:
+            for s in map_steps:
+                wait(s[t])
+                start(s[t + 1])
+        add_loads(arrival(t), False)
+    for k in range(max(n - 1, 2), len(bits)):
         for s in map_steps:
             wait(s[k - 1])
             start(s[k])
 
     here = dot(gface[...], loads[...].astype(BF))
-    take(last)
-    sent.extend(c_copies)
+    move_contrib(n - 1)
     here = (here + dot(gp, contrib[last])).astype(BF)
     faces[d, 0, pl.ds(z0, fr), :] = here[:fr]
     faces[d, 1, pl.ds(z0, fr), :] = here[fr:]
@@ -274,49 +323,13 @@
     vw = (dot(wc_h, inc) + dot(wc_l, inc)).astype(BF)
     ve = (dot(ec_h, outgoing) + dot(ec_l, outgoing)).astype(BF)
     sol[z] = (init[...] + dot(gsel[...], jnp.concatenate([vw, ve], axis=0))).astype(BF)
-    chunks = o_r.shape[1]
-    span = rows // chunks
-
-    def passing(block, c, way):
-        ref = sol.at[block, pl.ds(c * span, span), :]
-        return pltpu.make_async_remote_copy(
-            src_ref=ref, dst_ref=ref, send_sem=o_s.at[way, block, c], recv_sem=o_r.at[block, c],
-            device_id={"grp": z + 1 - 2 * way}, device_id_type=MESH)
-
-    def turn_index():
-        turned = jnp.transpose(idx_ref[...])
-        for r in range(nodes // 128):
-            column = turned[:, r:r + 1]
-
-            @pl.loop(0, interface // tile)
-            def _(i):
-                c0 = pl.multiple_of(i * tile, tile)
-                place = lax.broadcasted_iota(jnp.int32, (128, tile), 1) + c0
-                pt[r * 128:(r + 1) * 128, pl.ds(c0, tile)] = jnp.where(place == column, 1.0, 0.0).astype(BF)
-
     def add_picked(block):
         c0 = pl.multiple_of(block * rows, rows)
         return dot(pt[:, pl.ds(c0, rows)], sol[block])
 
-    can = (z < n - 1, z > 0)
-
-    def have(s, way):
-        return z >= s if way == 0 else z + s < n
-
     for s in range(n):
-        for c in range(chunks):
-            for way in range(2):
-                block = z - s if way == 0 else z + s
-                if s:
-                    @pl.when(have(s, way))
-                    def _():
-                        passing(block, c, way).wait_recv()
-
-                @pl.when(jnp.logical_and(have(s, way), can[way]))
-                def _():
-                    passing(block, c, way).start()
+        move_sol(s)
         if s == 0:
-            turn_index()
             picked[...] = add_picked(z)
             continue
         for way in range(2):
@@ -328,14 +341,8 @@
 
     for c in sent:
         c.wait_send()
-    for s in range(n - 1):
-        for c in range(chunks):
-            for way in range(2):
-                block = z - s if way == 0 else z + s
-
-                @pl.when(jnp.logical_and(have(s, way), can[way]))
-                def _():
-                    passing(block, c, way).wait_send()
+    end_contrib()
+    end_sol()
 
     out_ref[...] = (dot(lmt[...], picked[...].astype(BF)) + ll_ref[...].astype(F32)).astype(BF)
 
@@ -375,7 +382,7 @@
                 pltpu.VMEM((nodes, nodes), BF),
                 pltpu.VMEM((nodes, cols), F32),
                 pltpu.VMEM((interface, nodes), BF),
-                dma, dma((n,)), dma((n,)), dma((n,)), dma((n,)), dma((n,)), dma((n,)),
+                dma, dma((n,)), dma((n,)), dma((2, n, 2)), dma((n, 2)), dma((n,)), dma((n,)),
                 dma((n,)), dma((n,)), dma((2, n, 4)), dma((n, 4)),
                 dma((6, doms)), dma((6, doms)), dma((2, doms)), dma((2, doms)),
             ],

time: 93.2 us -> 80.2 us (0.86)
  Pallas kernels: 91.4 us -> 78.3 us
    pallas_call x1, Pallas kernels: 91.4 us -> 78.3 us  [on_device(): pl.pallas_call(functools.partial(kernel, n, doms), out_shape=jax.ShapeDty...]
where the time goes in v5:
time: 80.2 us; the launch traced here: 80 us
  Pallas kernels  78.3 us (98%)
  local copies, waits for them, and re-layouts  1.67 us (2%)
    pallas_call x1, Pallas kernels, on_device(): pl.pallas_call(functools.partial(kernel, n, doms), out_shape=jax.ShapeDty...  78.3 us
    unnamed x1, local copies, waits for them, and re-layouts  1.67 us

profile of v5, /device:TPU:0, one launch (start us, length us, event | category | flops | bytes accessed | tf_op | source)
XLA Modules:
  0.0 80.0 jit_solution(8798699013136109546)
XLA Ops:
  0.0 78.3 %shard_map.64 = bf16[1024,128]{1,0:T(8,128)(2,1)} custom-call(bf16[1024,1024]{1,0:T(8,128)(2,1)} %bitcast.9, bf16[1024,128]{1,0:T(8,128)(2,1)} %bitcast.10, bf16[1024,4096]{1,0:T(8,128)(2,1)} %bitcast.8, s32[8,128]{1,0:T(8,128)} %bitcast.13, f32[256,256]{1,0:T(8,128)} %bitcast.11, f32[256,256]{1,0:T(8,128)} %bitcast.12), custom_call_target="tpu_custom_call" | custom-call | flops 10000000000 | bytes 11000000 | tf_op jit(solution)/shard_map/pallas_call | solution.py:360
  78.3 1.7 %copy.8 = bf16[1,1,1024,128]{3,2,1,0:T(8,128)(2,1)} copy(bf16[1,1,1024,128]{3,2,1,0:T(8,128)(2,1)} %bitcast.7) | data formatting | bytes 524288

commit v6 on v5

--- a/solution.py
+++ b/solution.py
@@ -87,12 +87,11 @@
     def have(s, way):
         return z >= s if way == 0 else z + s < n
 
-    def line(buf, ss, rs):
+    def line(part, ss, rs):
         chunks = rs.shape[1]
-        span = buf.shape[1] // chunks
 
         def passing(block, c, way):
-            ref = buf.at[block, pl.ds(c * span, span), :]
+            ref = part(block, c, chunks)
             return pltpu.make_async_remote_copy(
                 src_ref=ref, dst_ref=ref, send_sem=ss.at[way, block, c], recv_sem=rs.at[block, c],
                 device_id={"grp": z + 1 - 2 * way}, device_id_type=MESH)
@@ -122,8 +121,16 @@
 
         return move, end
 
-    move_contrib, end_contrib = line(contrib, c_s, c_r)
-    move_sol, end_sol = line(sol, o_s, o_r)
+    def whole_block(buf):
+        return lambda block, c, chunks: buf.at[block, pl.ds(c * (buf.shape[1] // chunks), buf.shape[1] // chunks), :]
+
+    def face_block(buf):
+        return lambda block, c, chunks: buf.at[d, :, pl.ds(pl.multiple_of(block * fr, fr), fr), :]
+
+    move_contrib, end_contrib = line(whole_block(contrib), c_s, c_r)
+    move_sol, end_sol = line(whole_block(sol), o_s, o_r)
+    move_maps, end_maps = line(face_block(maps), m_s, m_r)
+    move_faces, end_faces = line(face_block(faces), f_s, f_r)
     i_copies = to_group(idx_all.at[z], i_s, i_r)
     start(i_copies)
 
@@ -159,9 +166,7 @@
     maps[d, 0, pl.ds(z0, fr), :] = forward[:fr].astype(BF)
     maps[d, 1, pl.ds(z0, fr), :] = forward[fr:].astype(BF)
     maps[d, 2, pl.ds(z0, fr), :] = backward.astype(BF)
-    m_copies = to_group(maps.at[d, :, pl.ds(z0, fr), :], m_s, m_r)
-    start(m_copies)
-
+    move_maps(0)
     move_contrib(0)
 
     place = lax.broadcasted_iota(jnp.int32, (tile, 128), 0).astype(jnp.int16)
@@ -220,8 +225,10 @@
 
     wait(i_copies)
     add_loads(z, True)
+    move_maps(1)
     turn_index()
-    wait(m_copies)
+    for s in range(2, n):
+        move_maps(s)
     for s in map_steps:
         start(s[0])
 
@@ -258,15 +265,21 @@
     here = (here + dot(gp, contrib[last])).astype(BF)
     faces[d, 0, pl.ds(z0, fr), :] = here[:fr]
     faces[d, 1, pl.ds(z0, fr), :] = here[fr:]
-    f_copies = to_group(faces.at[d, :, pl.ds(z0, fr), :], f_s, f_r)
-    start(f_copies)
-
-    @pl.loop(0, interface // tile)
-    def _(i):
-        r0 = pl.multiple_of(i * tile, tile)
-        loads_b[pl.ds(r0, tile), :] = (loads[pl.ds(r0, tile), :] + dot(plast[pl.ds(r0, tile), :], contrib[last])).astype(BF)
-
-    wait(f_copies)
+    move_faces(0)
+
+    def end_loads(start, stop):
+        @pl.loop(start, stop)
+        def _(i):
+            r0 = pl.multiple_of(i * tile, tile)
+            rest = dot(plast[pl.ds(r0, tile), :], contrib[last])
+            loads_b[pl.ds(r0, tile), :] = (loads[pl.ds(r0, tile), :] + rest).astype(BF)
+
+    middle = interface // tile // 2
+    end_loads(0, middle)
+    move_faces(1)
+    end_loads(middle, interface // tile)
+    for s in range(2, n):
+        move_faces(s)
     for s in face_steps:
         start(s[0])
 
@@ -342,6 +355,8 @@
     for c in sent:
         c.wait_send()
     end_contrib()
+    end_maps()
+    end_faces()
     end_sol()
 
     out_ref[...] = (dot(lmt[...], picked[...].astype(BF)) + ll_ref[...].astype(F32)).astype(BF)
@@ -382,8 +397,8 @@
                 pltpu.VMEM((nodes, nodes), BF),
                 pltpu.VMEM((nodes, cols), F32),
                 pltpu.VMEM((interface, nodes), BF),
-                dma, dma((n,)), dma((n,)), dma((2, n, 2)), dma((n, 2)), dma((n,)), dma((n,)),
-                dma((n,)), dma((n,)), dma((2, n, 4)), dma((n, 4)),
+                dma, dma((n,)), dma((n,)), dma((2, n, 2)), dma((n, 2)), dma((2, n, 1)), dma((n, 1)),
+                dma((2, n, 1)), dma((n, 1)), dma((2, n, 4)), dma((n, 4)),
                 dma((6, doms)), dma((6, doms)), dma((2, doms)), dma((2, doms)),
             ],
             compiler_params=pltpu.CompilerParams(

time: 80.2 us -> 86.9 us (1.084)
  Pallas kernels: 78.3 us -> 85 us
    pallas_call x1, Pallas kernels: 78.3 us -> 85 us  [on_device(): pl.pallas_call(functools.partial(kernel, n, doms), out_shape=jax.ShapeDty...]
where the time goes in v6:
time: 86.9 us; the launch traced here: 86.7 us
  Pallas kernels  85 us (98%)
  local copies, waits for them, and re-layouts  1.67 us (2%)
    pallas_call x1, Pallas kernels, on_device(): pl.pallas_call(functools.partial(kernel, n, doms), out_shape=jax.ShapeDty...  85 us

profile of v6, /device:TPU:0, one launch (start us, length us, event | category | flops | bytes accessed | tf_op | source)
XLA Modules:
  0.0 86.7 jit_solution(10325892184153845763)
XLA Ops:
  0.0 85.0 %shard_map.64 = bf16[1024,128]{1,0:T(8,128)(2,1)} custom-call(bf16[1024,1024]{1,0:T(8,128)(2,1)} %bitcast.9, bf16[1024,128]{1,0:T(8,128)(2,1)} %bitcast.10, bf16[1024,4096]{1,0:T(8,128)(2,1)} %bitcast.8, s32[8,128]{1,0:T(8,128)} %bitcast.13, f32[256,256]{1,0:T(8,128)} %bitcast.11, f32[256,256]{1,0:T(8,128)} %bitcast.12), custom_call_target="tpu_custom_call" | custom-call | flops 10000000000 | bytes 11000000 | tf_op jit(solution)/shard_map/pallas_call | solution.py:375
  85.0 1.7 %copy.8 = bf16[1,1,1024,128]{3,2,1,0:T(8,128)(2,1)} copy(bf16[1,1,1024,128]{3,2,1,0:T(8,128)(2,1)} %bitcast.7) | data formatting | bytes 524288

commit v7 on v5

--- a/solution.py
+++ b/solution.py
@@ -382,7 +382,7 @@
                 pltpu.VMEM((nodes, nodes), BF),
                 pltpu.VMEM((nodes, cols), F32),
                 pltpu.VMEM((interface, nodes), BF),
-                dma, dma((n,)), dma((n,)), dma((2, n, 2)), dma((n, 2)), dma((n,)), dma((n,)),
+                dma, dma((n,)), dma((n,)), dma((2, n, 4)), dma((n, 4)), dma((n,)), dma((n,)),
                 dma((n,)), dma((n,)), dma((2, n, 4)), dma((n, 4)),
                 dma((6, doms)), dma((6, doms)), dma((2, doms)), dma((2, doms)),
             ],

time: 80.2 us -> 80.5 us (level)
  no operation moved by 1% of the time
where the time goes in v7:
time: 80.5 us; the launch traced here: 80.3 us
  Pallas kernels  78.6 us (98%)
  local copies, waits for them, and re-layouts  1.67 us (2%)
    pallas_call x1, Pallas kernels, on_device(): pl.pallas_call(functools.partial(kernel, n, doms), out_shape=jax.ShapeDty...  78.6 us
    unnamed x1, local copies, waits for them, and re-layouts  1.67 us

profile of v7, /device:TPU:0, one launch (start us, length us, event | category | flops | bytes accessed | tf_op | source)
XLA Modules:
  0.0 80.3 jit_solution(1118381621237072360)
XLA Ops:
  0.0 78.6 %shard_map.64 = bf16[1024,128]{1,0:T(8,128)(2,1)} custom-call(bf16[1024,1024]{1,0:T(8,128)(2,1)} %bitcast.9, bf16[1024,128]{1,0:T(8,128)(2,1)} %bitcast.10, bf16[1024,4096]{1,0:T(8,128)(2,1)} %bitcast.8, s32[8,128]{1,0:T(8,128)} %bitcast.13, f32[256,256]{1,0:T(8,128)} %bitcast.11, f32[256,256]{1,0:T(8,128)} %bitcast.12), custom_call_target="tpu_custom_call" | custom-call | flops 10000000000 | bytes 11000000 | tf_op jit(solution)/shard_map/pallas_call | solution.py:360
  78.6 1.7 %copy.8 = bf16[1,1,1024,128]{3,2,1,0:T(8,128)(2,1)} copy(bf16[1,1,1024,128]{3,2,1,0:T(8,128)(2,1)} %bitcast.7) | data formatting | bytes 524288
